TPU v7x, 32 devices: a whole 2x2x4 slice. The times are simulated.
32 devices in a mesh: grp: 2 (over y), mesh: 16 (over z, x, core).
Axes of the slice: x: 2, y: 2, z: 4, core: 2. Of those that a mesh axis runs over, the one named last changes fastest.
Arguments:
- basis: bfloat16 [65536, 512], P(('grp', 'mesh')), parts along dimension 0, may hold values from -6 to 6
- blocks: bfloat16 [2, 512, 3, 128, 128], P(None, ('grp', 'mesh')), parts along dimension 1, may hold values from -0.0017089844 to 0.0017089844
- columns: int32 [2, 512, 2], P(None, ('grp', 'mesh')), parts along dimension 1, may hold values from 0 to 31
- sends: int32 [32, 16], P(('grp', 'mesh')), parts along dimension 0, may hold values from 0 to 15
Outputs:
- projected: float32 [1024, 1024], P(('grp', 'mesh')), parts along dimension 0
There are 2 independent parts, one for each index of `grp`. A program takes and returns all parts, laid end to end along the dimension named above; each array names one. Nothing has to cross between parts.
All inputs are finite; a program needn't handle non-finite values.
Results may differ from a plain program's by a relative error of at most 0.0029.
Values may be sent and summed in bfloat16 or wider, within the bound.
No kernel may reach another device: no remote copies, remote signals or barrier semaphores. Data moves between devices by JAX's collectives and lax.ppermute only.
A program may use at most 64 MiB of HBM per device.

v0:
```python
import jax
import jax.numpy as jnp
from jax import lax
from jax.sharding import PartitionSpec as P


def from_behind(value, axis, steps):
    count = lax.axis_size(axis)
    leading, last = (max(0, -steps), min(count, count - steps))
    return lax.ppermute(value, axis, [(source, source + steps) for source in range(leading, last)])


def shards(basis, blocks, columns, sends):
    count_params, count_blocks, count_slots, block_size, _ = blocks.shape
    basis_width = basis.shape[1]
    halo_count = sends.shape[1] // 2
    own_blocks = basis.reshape(count_blocks, block_size, basis_width)
    diag_index = jnp.arange(count_blocks, dtype=jnp.int32)[:, None]
    images = []
    upward = jnp.take(own_blocks, sends[0, halo_count:], axis=0)
    downward = jnp.take(own_blocks, sends[0, :halo_count], axis=0)
    from_below = from_behind(upward, "mesh", 1)
    from_above = from_behind(downward, "mesh", -1)
    extended = jnp.concatenate([own_blocks, from_below, from_above], axis=0)
    for param in range(count_params):
        slot_index = jnp.concatenate([diag_index, columns[param]], axis=1)
        gathered = jnp.take(extended, slot_index, axis=0)
        accumulated = jnp.einsum(
            "bsik,bskj->bij", blocks[param], gathered, preferred_element_type=jnp.float32
        )
        images.append(
            accumulated.astype(jnp.bfloat16).reshape(count_blocks * block_size, basis_width)
        )
    stacked_images = jnp.concatenate(images, axis=1)
    return lax.psum_scatter(
        lax.dot_general(
            basis, stacked_images, (((0,), (0,)), ((), ())), preferred_element_type=jnp.float32
        ),
        "mesh",
        scatter_dimension=0,
        tiled=True,
    )


def solution(mesh):
    placed = (
        P(("grp", "mesh"), None),
        P(None, ("grp", "mesh"), None, None, None),
        P(None, ("grp", "mesh"), None),
        P(("grp", "mesh"), None),
    )
    return jax.shard_map(
        shards, mesh=mesh, in_specs=placed, out_specs=P(("grp", "mesh"), None), check_vma=False
    )
```

profile of v0, /device:TPU:0, one launch (start us, length us, event | category | flops | bytes accessed | tf_op | source)
XLA Modules:
  0.0 141.1 jit_solution(12706131674554391843)
XLA Ops:
  6.5 0.0 copy-start
  6.5 0.0 reduce-scatter.4.cloned.1.call-start
  6.5 0.9 compare_and_fusion.3
  7.4 0.0 copy-start.2
  7.5 2.2 %gather_fusion = bf16[8,128,512]{2,1,0:T(8,128)(2,1)S(1)} fusion(bf16[16,128,512]{2,1,0:T(8,128)(2,1)} %bitcast.35, s32[1024]{0:T(1024)S(1)} %pad_clamp_fusion.3), kind=kCustom, calls=%fused_computation.clone | custom fusion | bytes 2097184 | tf_op jit(solution)/shard_map/jit(_take)/gather | solution.py:20
  9.7 1.2 broadcast_select_fusion.1
  10.9 3.3 %collective-permute-start = (bf16[8,128,512]{2,1,0:T(8,128)(2,1)}, bf16[8,128,512]{2,1,0:T(8,128)(2,1)}, u32[]{:S(2)}, u32[]{:S(2)}) collective-permute-start(bf16[8,128,512]{2,1,0:T(8,128)(2,1)} %broadcast_select_fusion.1), channel_id=1, source_target_pairs={{0,1},{1,2},{2,3},{3,4},{4,5},{5,6},{6,7},{7,8},{8,9},{9,10},{10,1... | collective-permute-start | bytes 3145736 | tf_op jit(solution)/shard_map/ppermute | solution.py:10
  14.2 0.0 copy-done
  14.2 0.6 gather_fusion.1
  14.8 1.2 broadcast_select_fusion
  16.0 1.3 collective-permute-start.1
  17.3 0.0 copy-done.2
  17.3 0.1 copy.16
  17.4 0.1 reshape.64
  17.5 0.1 copy.15
  17.6 0.1 copy.18
  17.7 0.1 reshape.68
  17.8 0.1 copy.17
  17.9 0.0 collective-permute-done
  17.9 4.0 %collective-permute-done.1 = bf16[8,128,512]{2,1,0:T(8,128)(2,1)S(1)} collective-permute-done((bf16[8,128,512]{2,1,0:T(8,128)(2,1)}, bf16[8,128,512]{2,1,0:T(8,128)(2,1)S(1)}, u32[]{:S(2)}, u32[]{:S(2)}) %collective-permute-start.1) | collective-permute-done | bytes 1048608 | tf_op jit(solution)/shard_map/ppermute | solution.py:10
  21.9 3.5 %pad_maximum_fusion = bf16[32,128,512]{2,1,0:T(8,128)(2,1)} fusion(bf16[8,128,512]{2,1,0:T(8,128)(2,1)S(1)} %collective-permute-done.1, bf16[8,128,512]{2,1,0:T(8,128)(2,1)} %collective-permute-done, bf16[16,128,512]{2,1,0:T(8,128)(2,1)S(1)} %bitcast.37), kind=kLoop, calls=%fused_computation.10 | loop fusion | flops 4194304 | bytes 8388608 | tf_op jit(solution)/shard_map/concatenate | solution.py:24
  25.4 7.2 %gather_fusion.2 = bf16[48,128,512]{2,1,0:T(8,128)(2,1)} fusion(bf16[32,128,512]{2,1,0:T(8,128)(2,1)} %pad_maximum_fusion, s32[1024]{0:T(1024)S(1)} %pad_clamp_fusion.1), kind=kCustom, calls=%fused_computation.1.clone | custom fusion | bytes 12583104 | tf_op jit(solution)/shard_map/jit(_take)/gather | solution.py:27
  32.5 7.2 %gather_fusion.3 = bf16[48,128,512]{2,1,0:T(8,128)(2,1)} fusion(bf16[32,128,512]{2,1,0:T(8,128)(2,1)} %pad_maximum_fusion, s32[1024]{0:T(1024)S(1)} %pad_clamp_fusion), kind=kCustom, calls=%fused_computation.3.clone | custom fusion | bytes 12583104 | tf_op jit(solution)/shard_map/jit(_take)/gather | solution.py:27
  39.7 0.0 copy-start.1
  39.7 0.0 copy-start.3
  39.7 4.8 %bitcast_convert_fusion.1 = bf16[16,512,128]{1,2,0:T(8,128)(2,1)S(1)} fusion(bf16[16,3,128,512]{3,2,1,0:T(8,128)(2,1)} %bitcast.39, pred[16,3]{1,0:T(8,128)(4,1)S(1)} %copy.15, bf16[2,16,3,128,128]{4,3,2,1,0:T(8,128)(2,1)} %param.9), kind=kOutput, calls=%fused_computation.16 | convolution fusion | flops 809500672 | bytes 9961520 | tf_op jit(solution)/shard_map/bsik,bskj->bij/dot_general | solution.py:28
  44.5 0.2 copy-done.1
  44.8 0.9 copy-done.3
  45.7 1.6 %bitcast_convert_fusion = bf16[16,512,128]{1,2,0:T(8,128)(2,1)S(1)} fusion(bf16[16,3,128,512]{3,2,1,0:T(8,128)(2,1)S(1)} %bitcast.38, pred[16,3]{1,0:T(8,128)(4,1)S(1)} %copy.17, bf16[2,16,3,128,128]{4,3,2,1,0:T(8,128)(2,1)S(1)} %copy-done.3), kind=kOutput, calls=%fused_computation.15 | convolution fusion | flops 809500672 | bytes 9963520 | tf_op jit(solution)/shard_map/bsik,bskj->bij/dot_general | solution.py:28
  47.3 3.7 %fusion.16 = f32[512,1024]{0,1:T(8,128)} fusion(bf16[2048,512]{1,0:T(8,128)(2,1)S(1)} %copy-done, bf16[2048,512]{1,0:T(8,128)(2,1)S(1)} %bitcast.41, bf16[2048,512]{1,0:T(8,128)(2,1)S(1)} %bitcast.40), kind=kOutput, calls=%fused_computation.19 | convolution fusion | flops 2155872256 | bytes 8388608 | tf_op jit(solution)/shard_map/dot_general | solution.py:36
  51.0 2.9 %copy.22 = f32[512,1024]{1,0:T(8,128)} copy(f32[512,1024]{0,1:T(8,128)} %fusion.16) | data formatting | bytes 4194304
  53.9 0.0 reduce-scatter.4.cloned.1.call-update
  53.9 80.4 %reduce-scatter.4.cloned.1.call-done = f32[32,1024]{1,0:T(8,128)} async-done(((f32[512,1024]{1,0:T(8,128)}), f32[32,1024]{1,0:T(8,128)}) %reduce-scatter.4.cloned.1.call-update) | async-done | bytes 131088 | tf_op jit(solution)/shard_map/reduce_scatter | solution.py:35
  (8 shorter events, 0.1 us)
Async XLA Ops:
  6.5 7.7 %copy-start = (bf16[2048,512]{1,0:T(8,128)(2,1)S(1)}, bf16[2048,512]{1,0:T(8,128)(2,1)}, u32[]{:S(2)}) copy-start(bf16[2048,512]{1,0:T(8,128)(2,1)} %param.8) | copy-start | bytes 6291460
  6.5 127.7 %reduce-scatter.4.cloned.1.call-start = ((), (), s32[]{:S(2)}) async-start(), calls=%async_computation.1 | async-start | bytes 2228224 | tf_op jit(solution)/shard_map/reduce_scatter | solution.py:35
  7.4 9.8 %copy-start.2 = (s32[2,16,2]{1,2,0:T(2,128)S(1)}, s32[2,16,2]{1,2,0:T(2,128)}, u32[]{:S(2)}) copy-start(s32[2,16,2]{1,2,0:T(2,128)} %param.10) | copy-start | bytes 772
  10.9 7.0 %collective-permute-start = (bf16[8,128,512]{2,1,0:T(8,128)(2,1)}, bf16[8,128,512]{2,1,0:T(8,128)(2,1)}, u32[]{:S(2)}, u32[]{:S(2)}) collective-permute-start(bf16[8,128,512]{2,1,0:T(8,128)(2,1)} %broadcast_select_fusion.1), channel_id=1, source_target_pairs={{0,1},{1,2},{2,3},{3,4},{4,5},{5,6},{6,7},{7,8},{8,9},{9,10},{10,1... | collective-permute-start | bytes 3145736 | tf_op jit(solution)/shard_map/ppermute | solution.py:10
  16.0 5.9 %collective-permute-start.1 = (bf16[8,128,512]{2,1,0:T(8,128)(2,1)}, bf16[8,128,512]{2,1,0:T(8,128)(2,1)S(1)}, u32[]{:S(2)}, u32[]{:S(2)}) collective-permute-start(bf16[8,128,512]{2,1,0:T(8,128)(2,1)} %broadcast_select_fusion), channel_id=1, source_target_pairs={{1,0},{2,1},{3,2},{4,3},{5,4},{6,5},{7,6},{8,7},{9,8},{10,9},{11,1... | collective-permute-start | bytes 3145736 | tf_op jit(solution)/shard_map/ppermute | solution.py:10
  39.7 5.0 %copy-start.1 = (bf16[48,128,512]{2,1,0:T(8,128)(2,1)S(1)}, bf16[48,128,512]{2,1,0:T(8,128)(2,1)}, u32[]{:S(2)}) copy-start(bf16[48,128,512]{2,1,0:T(8,128)(2,1)} %gather_fusion.3) | copy-start | bytes 18874372
  39.7 6.0 %copy-start.3 = (bf16[2,16,3,128,128]{4,3,2,1,0:T(8,128)(2,1)S(1)}, bf16[2,16,3,128,128]{4,3,2,1,0:T(8,128)(2,1)}, u32[]{:S(2)}) copy-start(bf16[2,16,3,128,128]{4,3,2,1,0:T(8,128)(2,1)} %param.9) | copy-start | bytes 9437188
Sparse Core Ops, SparseCore 0:
  54.0 80.2 reduce-scatter.3
where the time goes:
time: 141 us
  waiting for transfers between devices  84.4 us (60%)
  local copies, waits for them, and re-layouts  21.7 us (15%)
  between operations  13.5 us (10%)
  matrix products  10.1 us (7%)
  other arithmetic  6.8 us (5%)
  starting transfers between devices  4.61 us (3%)
    reduce_scatter x1, waiting for transfers between devices, shards(): lax.psum_scatter(lax.dot_general(basis, stacked_images, (((0,), (0,)), ((...  80.4 us
    gather x2, local copies, waits for them, and re-layouts, shards(): gathered = jnp.take(extended, slot_index, axis=0)  14.3 us
    dot_general x2, matrix products, shards(): jnp.einsum('bsik,bskj->bij', blocks[param], gathered, preferred_element_t...  6.39 us
    ppermute x2, starting transfers between devices, from_behind(): lax.ppermute(value, axis, [(source, source + steps) for source in range(l...  4.61 us
    unnamed x9, local copies, waits for them, and re-layouts  4.05 us
    ppermute x2, waiting for transfers between devices, from_behind(): lax.ppermute(value, axis, [(source, source + steps) for source in range(l...  3.97 us
    dot_general x1, matrix products, shards(): lax.dot_general(basis, stacked_images, (((0,), (0,)), ((), ())), preferre...  3.69 us
    concatenate x1, other arithmetic, shards(): extended = jnp.concatenate([own_blocks, from_below, from_above], axis=0)  3.52 us
  transfers between devices with their start and end apart: 3, of which 2 were waited for; matrix products, arithmetic and copies ran while one was open for 2% of the time, Pallas kernels for 0%

commit v1 on v0

v1 whole, which is shorter than its diff:
```python
import jax
import jax.numpy as jnp
from jax import lax
from jax.sharding import PartitionSpec as P

AXIS = "mesh"


def pairs(count, first):
    both = []
    for low in range(first, count - 1, 2):
        both += [(low, low + 1), (low + 1, low)]
    return both


def shards(basis, blocks, columns, sends):
    count_params, count_blocks, count_slots, block_size, _ = blocks.shape
    width = basis.shape[1]
    halo = sends.shape[1] // 2
    count = lax.axis_size(AXIS)
    odd = lax.rem(lax.axis_index(AXIS), 2)
    own = basis.reshape(count_blocks, block_size, width)

    lists = sends.reshape(2, halo)
    far = jnp.take(own, lists[odd], axis=0, mode="clip")
    near = jnp.take(own, lists[1 - odd], axis=0, mode="clip")
    from_far = lax.ppermute(far, AXIS, pairs(count, 1))
    from_near = lax.ppermute(near, AXIS, pairs(count, 0))
    lower = jnp.where(odd == 0, from_far, from_near)
    upper = jnp.where(odd == 0, from_near, from_far)
    extended = jnp.concatenate([own, lower, upper], axis=0)

    diagonal = jnp.arange(count_blocks, dtype=jnp.int32)[:, None]
    images = []
    for param in range(count_params):
        index = jnp.concatenate([diagonal, columns[param]], axis=1)
        gathered = jnp.take(extended, index, axis=0, mode="clip")
        image = jnp.einsum(
            "bsik,bskj->bij", blocks[param], gathered, preferred_element_type=jnp.float32
        )
        images.append(image.astype(jnp.bfloat16).reshape(count_blocks * block_size, width))
    stacked = jnp.concatenate(images, axis=1)
    partial = lax.dot_general(
        basis, stacked, (((0,), (0,)), ((), ())), preferred_element_type=jnp.float32
    )
    chips = count // 2
    rows = partial.shape[0] // count
    partial = partial.reshape(chips, 2, rows, partial.shape[1])
    keep = lax.dynamic_index_in_dim(partial, odd, axis=1, keepdims=False)
    give = lax.dynamic_index_in_dim(partial, 1 - odd, axis=1, keepdims=False)
    taken = lax.ppermute(give.astype(jnp.bfloat16), AXIS, pairs(count, 0))
    chip_sum = (keep + taken.astype(jnp.float32)).astype(jnp.bfloat16)
    groups = [list(range(core, count, 2)) for core in range(2)]
    parts = lax.all_to_all(
        chip_sum, AXIS, split_axis=0, concat_axis=0, axis_index_groups=groups, tiled=True
    )
    return jnp.sum(parts.astype(jnp.float32), axis=0)


def solution(mesh):
    placed = (
        P(("grp", "mesh"), None),
        P(None, ("grp", "mesh"), None, None, None),
        P(None, ("grp", "mesh"), None),
        P(("grp", "mesh"), None),
    )
    return jax.shard_map(
        shards, mesh=mesh, in_specs=placed, out_specs=P(("grp", "mesh"), None), check_vma=False
    )
```

time: 141 us -> 84.3 us (0.60)
  waiting for transfers between devices: 84.4 us -> 3.76 us
  blocking collectives: 0 us -> 20.5 us
  starting transfers between devices: 4.61 us -> 22.4 us
  between operations: 13.5 us -> 0.12 us
  matrix products: 10.1 us -> 8.27 us
  local copies, waits for them, and re-layouts: 21.7 us -> 23.2 us
    reduce_scatter x1 -> x0, waiting for transfers between devices: 80.4 us -> none  [shards(): lax.psum_scatter(lax.dot_general(basis, stacked_images, (((0,), (0,)), ((...]
    all_to_all x0 -> x1, blocking collectives: none -> 20.5 us  [shards(): lax.all_to_all(chip_sum, AXIS, split_axis=0, concat_axis=0, axis_index_gr...]
    ppermute x2 -> x3, starting transfers between devices: 4.61 us -> 22.4 us  [the longest x1 17.5 us: shards(): taken = lax.ppermute(give.astype(jnp.bfloat16), AXIS, pairs(count, 0))]
    gather x4, local copies, waits for them, and re-layouts: 17.1 us -> 20.8 us  [the longest x2 14.3 us: shards(): gathered = jnp.take(extended, index, axis=0, mode='clip')]
    unnamed x9, local copies, waits for them, and re-layouts: 4.05 us -> 1.83 us
    concatenate x1 -> x2, other arithmetic: 3.52 us -> 2.2 us  [the longest x1 2.19 us: shards(): extended = jnp.concatenate([own, lower, upper], axis=0)]
    ppermute x2 -> x3, waiting for transfers between devices: 3.97 us -> 3.76 us  [the longest x1 2.22 us: shards(): from_near = lax.ppermute(near, AXIS, pairs(count, 0))]
  transfers between devices with their start and end apart: 3 -> 3, of which waited for: 2 -> 2; matrix products, arithmetic and copies ran while one was open for 2% -> 4% of each run, Pallas kernels for 0% -> 0%
where the time goes in v1:
time: 84.3 us; the launch traced here: 84 us
  local copies, waits for them, and re-layouts  23.2 us (28%)
  starting transfers between devices  22.4 us (27%)
  blocking collectives  20.5 us (24%)
  matrix products  8.27 us (10%)
  other arithmetic  5.78 us (7%)
  waiting for transfers between devices  3.76 us (4%)
    all_to_all x1, blocking collectives, shards(): lax.all_to_all(chip_sum, AXIS, split_axis=0, concat_axis=0, axis_index_gr...  20.5 us
    ppermute x1, starting transfers between devices, shards(): taken = lax.ppermute(give.astype(jnp.bfloat16), AXIS, pairs(count, 0))  17.5 us
    gather x2, local copies, waits for them, and re-layouts, shards(): gathered = jnp.take(extended, index, axis=0, mode='clip')  14.3 us
    dot_general x2, matrix products, shards(): jnp.einsum('bsik,bskj->bij', blocks[param], gathered, preferred_element_t...  5.91 us
    ppermute x1, starting transfers between devices, shards(): from_near = lax.ppermute(near, AXIS, pairs(count, 0))  4.23 us
    gather x1, local copies, waits for them, and re-layouts, shards(): far = jnp.take(own, lists[odd], axis=0, mode='clip')  3.33 us
    gather x1, local copies, waits for them, and re-layouts, shards(): near = jnp.take(own, lists[1 - odd], axis=0, mode='clip')  3.23 us
    dot_general x1, matrix products, shards(): lax.dot_general(basis, stacked, (((0,), (0,)), ((), ())), preferred_eleme...  2.36 us
  transfers between devices with their start and end apart: 3, of which 2 were waited for; matrix products, arithmetic and copies ran while one was open for 4% of the time, Pallas kernels for 0%

profile of v1, /device:TPU:0, one launch (start us, length us, event | category | flops | bytes accessed | tf_op | source)
XLA Modules:
  0.0 84.0 jit_solution(16547436280189742094)
XLA Ops:
  0.0 0.0 copy-start.3
  0.0 0.5 broadcast.20
  0.5 1.3 %reduce.3 = s32[16]{0:T(128)S(1)} reduce(s32[1,16]{1,0:T(1,128)} %param.7, s32[]{:T(128)} %broadcast.20), dimensions={0}, to_apply=%param.7.reduce_sub_computation.3 | reduce | bytes 132 | tf_op args[3]
  1.8 0.1 reshape.19
  1.9 0.0 copy-start.1
  1.9 3.3 %gather_fusion = bf16[8,128,512]{2,1,0:T(8,128)(2,1)} fusion(bf16[16,128,512]{2,1,0:T(8,128)(2,1)} %bitcast.43, s32[1024]{0:T(1024)S(1)} %pad_clamp_fusion.3), kind=kCustom, calls=%fused_computation | custom fusion | bytes 2097184 | tf_op jit(solution)/shard_map/jit(_take)/gather | solution.py:25
  5.3 0.7 collective-permute-start
  6.0 3.2 %gather_fusion.1 = bf16[8,128,512]{2,1,0:T(8,128)(2,1)} fusion(bf16[16,128,512]{2,1,0:T(8,128)(2,1)} %bitcast.44, s32[1024]{0:T(1024)S(1)} %pad_clamp_fusion.2), kind=kCustom, calls=%fused_computation.1 | custom fusion | bytes 2097184 | tf_op jit(solution)/shard_map/jit(_take)/gather | solution.py:26
  9.2 4.2 %collective-permute-start.1 = (bf16[8,128,512]{2,1,0:T(8,128)(2,1)}, bf16[8,128,512]{2,1,0:T(8,128)(2,1)}, u32[]{:S(2)}, u32[]{:S(2)}) collective-permute-start(bf16[8,128,512]{2,1,0:T(8,128)(2,1)} %gather_fusion.1), channel_id=1, source_target_pairs={{0,1},{1,0},{2,3},{3,2},{4,5},{5,4},{6,7},{7,6},{8,9},{9,8},{10,11... | collective-permute-start | bytes 3145736 | tf_op jit(solution)/shard_map/ppermute | solution.py:28
  13.5 0.0 copy-done.3
  13.5 0.1 copy.7
  13.6 0.1 reshape.41
  13.7 0.1 copy.8
  13.8 0.1 reshape.49
  13.9 0.0 collective-permute-done
  13.9 2.2 %collective-permute-done.1 = bf16[8,128,512]{2,1,0:T(8,128)(2,1)} collective-permute-done((bf16[8,128,512]{2,1,0:T(8,128)(2,1)}, bf16[8,128,512]{2,1,0:T(8,128)(2,1)}, u32[]{:S(2)}, u32[]{:S(2)}) %collective-permute-start.1) | collective-permute-done | bytes 1048608 | tf_op jit(solution)/shard_map/ppermute | solution.py:28
  16.1 1.4 %broadcast_select_fusion.1 = (bf16[8,128,512]{2,1,0:T(8,128)(2,1)S(1)}, bf16[8,128,512]{2,1,0:T(8,128)(2,1)S(1)}) fusion(bf16[8,128,512]{2,1,0:T(8,128)(2,1)S(1)} %collective-permute-done, bf16[8,128,512]{2,1,0:T(8,128)(2,1)} %collective-permute-done.1, pred[]{:T(512)S(6)} %eq.4), kind=kLoop, calls=%fused_computation.20 | loop fusion | flops 1048576 | bytes 4194305 | tf_op jit(solution)/shard_map/jit(_where)/select_n | solution.py:29
  17.5 0.0 copy-done.1
  17.5 2.2 %pad_maximum_fusion = bf16[32,128,512]{2,1,0:T(8,128)(2,1)} fusion(bf16[8,128,512]{2,1,0:T(8,128)(2,1)S(1)} %get-tuple-element.6, bf16[8,128,512]{2,1,0:T(8,128)(2,1)S(1)} %get-tuple-element.5, bf16[16,128,512]{2,1,0:T(8,128)(2,1)S(1)} %bitcast.45), kind=kLoop, calls=%fused_computation.4 | loop fusion | flops 4194304 | bytes 8388608 | tf_op jit(solution)/shard_map/concatenate | solution.py:31
  19.7 7.1 %gather_fusion.3 = bf16[48,128,512]{2,1,0:T(8,128)(2,1)} fusion(bf16[32,128,512]{2,1,0:T(8,128)(2,1)} %pad_maximum_fusion, s32[1024]{0:T(1024)S(1)} %pad_clamp_fusion), kind=kCustom, calls=%fused_computation.3 | custom fusion | bytes 12583104 | tf_op jit(solution)/shard_map/jit(_take)/gather | solution.py:37
  26.8 7.1 %gather_fusion.2 = bf16[48,128,512]{2,1,0:T(8,128)(2,1)} fusion(bf16[32,128,512]{2,1,0:T(8,128)(2,1)} %pad_maximum_fusion, s32[1024]{0:T(1024)S(1)} %pad_clamp_fusion.1), kind=kCustom, calls=%fused_computation.2 | custom fusion | bytes 12583104 | tf_op jit(solution)/shard_map/jit(_take)/gather | solution.py:37
  33.9 0.0 copy-start
  34.0 0.0 copy-start.2
  34.0 4.7 %bitcast_convert_fusion = bf16[16,512,128]{1,2,0:T(8,128)(2,1)S(1)} fusion(bf16[16,3,128,512]{3,2,1,0:T(8,128)(2,1)} %bitcast.41, bf16[2,16,3,128,128]{4,3,2,1,0:T(8,128)(2,1)} %param.5), kind=kOutput, calls=%fused_computation.9 | convolution fusion | flops 806354944 | bytes 9961472 | tf_op jit(solution)/shard_map/bsik,bskj->bij/dot_general | solution.py:38
  38.6 0.4 copy-done
  39.0 0.9 %copy-done.2 = bf16[2,16,3,128,128]{4,3,2,1,0:T(8,128)(2,1)S(1)} copy-done((bf16[2,16,3,128,128]{4,3,2,1,0:T(8,128)(2,1)S(1)}, bf16[2,16,3,128,128]{4,3,2,1,0:T(8,128)(2,1)}, u32[]{:S(2)}) %copy-start.2) | copy-done | bytes 3145752
  39.9 1.3 %bitcast_convert_fusion.1 = bf16[16,512,128]{1,2,0:T(8,128)(2,1)S(1)} fusion(bf16[16,3,128,512]{3,2,1,0:T(8,128)(2,1)S(1)} %bitcast.42, bf16[2,16,3,128,128]{4,3,2,1,0:T(8,128)(2,1)S(1)} %copy-done.2), kind=kOutput, calls=%fused_computation.10 | convolution fusion | flops 806354944 | bytes 9961472 | tf_op jit(solution)/shard_map/bsik,bskj->bij/dot_general | solution.py:38
  41.2 2.4 %fusion = f32[1024,512]{0,1:T(8,128)S(1)} fusion(bf16[2048,512]{1,0:T(8,128)(2,1)S(1)} %copy-done.1, bf16[2048,512]{1,0:T(8,128)(2,1)S(1)} %bitcast.46, bf16[2048,512]{1,0:T(8,128)(2,1)S(1)} %bitcast.47), kind=kOutput, calls=%fused_computation.5 | convolution fusion | flops 2155872256 | bytes 8388608 | tf_op jit(solution)/shard_map/dot_general | solution.py:43
  43.5 0.1 fusion.9
  43.6 17.5 %collective-permute-start.2 = (bf16[8,32,1024]{2,1,0:T(8,128)(2,1)S(1)}, bf16[8,32,1024]{2,1,0:T(8,128)(2,1)S(1)}, u32[]{:S(2)}, u32[]{:S(2)}) collective-permute-start(bf16[8,32,1024]{2,1,0:T(8,128)(2,1)S(1)} %fusion.9), channel_id=1, source_target_pairs={{0,1},{1,0},{2,3},{3,2},{4,5},{5,4},{6,7},{7,6},{8,9},{9,8},{10,11... | collective-permute-start | bytes 1572872 | tf_op jit(solution)/shard_map/ppermute | solution.py:51
  61.1 1.5 %collective-permute-done.2 = bf16[8,32,1024]{2,1,0:T(8,128)(2,1)S(1)} collective-permute-done((bf16[8,32,1024]{2,1,0:T(8,128)(2,1)S(1)}, bf16[8,32,1024]{2,1,0:T(8,128)(2,1)S(1)}, u32[]{:S(2)}, u32[]{:S(2)}) %collective-permute-start.2) | collective-permute-done | bytes 524320 | tf_op jit(solution)/shard_map/ppermute | solution.py:51
  62.6 0.1 fusion.8
  62.8 20.5 %all_to_all.5 = bf16[8,32,1024]{2,1,0:T(8,128)(2,1)S(1)} all-to-all(bf16[8,32,1024]{2,1,0:T(8,128)(2,1)S(1)} %fusion.8), channel_id=1, replica_groups={{0,2,4,6,8,10,12,14},{1,3,5,7,9,11,13,15},{16,18,20,22,24,26,28,30},{17..., dimensions={0} | all-to-all | bytes 1048576 | tf_op jit(solution)/shard_map/all_to_all | solution.py:54
  83.3 0.7 convert_reduce_fusion
  (8 shorter events, 0.0 us)
Async XLA Ops:
  0.0 13.5 %copy-start.3 = (s32[2,16,2]{1,2,0:T(2,128)S(1)}, s32[2,16,2]{1,2,0:T(2,128)}, u32[]{:S(2)}) copy-start(s32[2,16,2]{1,2,0:T(2,128)} %param.6) | copy-start | bytes 772
  1.9 15.5 %copy-start.1 = (bf16[2048,512]{1,0:T(8,128)(2,1)S(1)}, bf16[2048,512]{1,0:T(8,128)(2,1)}, u32[]{:S(2)}) copy-start(bf16[2048,512]{1,0:T(8,128)(2,1)} %param.4) | copy-start | bytes 6291460
  5.3 8.6 %collective-permute-start = (bf16[8,128,512]{2,1,0:T(8,128)(2,1)}, bf16[8,128,512]{2,1,0:T(8,128)(2,1)S(1)}, u32[]{:S(2)}, u32[]{:S(2)}) collective-permute-start(bf16[8,128,512]{2,1,0:T(8,128)(2,1)} %gather_fusion), channel_id=1, source_target_pairs={{1,2},{2,1},{3,4},{4,3},{5,6},{6,5},{7,8},{8,7},{9,10},{10,9},{11,... | collective-permute-start | bytes 3145736 | tf_op jit(solution)/shard_map/ppermute | solution.py:27
  9.2 6.9 %collective-permute-start.1 = (bf16[8,128,512]{2,1,0:T(8,128)(2,1)}, bf16[8,128,512]{2,1,0:T(8,128)(2,1)}, u32[]{:S(2)}, u32[]{:S(2)}) collective-permute-start(bf16[8,128,512]{2,1,0:T(8,128)(2,1)} %gather_fusion.1), channel_id=1, source_target_pairs={{0,1},{1,0},{2,3},{3,2},{4,5},{5,4},{6,7},{7,6},{8,9},{9,8},{10,11... | collective-permute-start | bytes 3145736 | tf_op jit(solution)/shard_map/ppermute | solution.py:28
  33.9 5.0 %copy-start = (bf16[48,128,512]{2,1,0:T(8,128)(2,1)S(1)}, bf16[48,128,512]{2,1,0:T(8,128)(2,1)}, u32[]{:S(2)}) copy-start(bf16[48,128,512]{2,1,0:T(8,128)(2,1)} %gather_fusion.2) | copy-start | bytes 18874372
  34.0 6.0 %copy-start.2 = (bf16[2,16,3,128,128]{4,3,2,1,0:T(8,128)(2,1)S(1)}, bf16[2,16,3,128,128]{4,3,2,1,0:T(8,128)(2,1)}, u32[]{:S(2)}) copy-start(bf16[2,16,3,128,128]{4,3,2,1,0:T(8,128)(2,1)} %param.5) | copy-start | bytes 9437188
  43.6 19.0 %collective-permute-start.2 = (bf16[8,32,1024]{2,1,0:T(8,128)(2,1)S(1)}, bf16[8,32,1024]{2,1,0:T(8,128)(2,1)S(1)}, u32[]{:S(2)}, u32[]{:S(2)}) collective-permute-start(bf16[8,32,1024]{2,1,0:T(8,128)(2,1)S(1)} %fusion.9), channel_id=1, source_target_pairs={{0,1},{1,0},{2,3},{3,2},{4,5},{5,4},{6,7},{7,6},{8,9},{9,8},{10,11... | collective-permute-start | bytes 1572872 | tf_op jit(solution)/shard_map/ppermute | solution.py:51
